TPU v7x, 256 devices: a whole 4x4x8 slice. The times are simulated.
256 devices in a mesh: row: 4 (over y), col: 16 (over z, core), layer: 4 (over x).
Axes of the slice: x: 4, y: 4, z: 8, core: 2. Of those that a mesh axis runs over, the one named last changes fastest.
Arguments:
- factor: bfloat16 [8192, 8192], P('layer', ('row', 'col')), as said below
- adjoint: bfloat16 [8192, 8192], P('layer', ('col', 'row')), as said below
- pattern: int32 [64, 64], replicated, may hold values from 0 to 1, as said below
Outputs:
- image: bfloat16 [8192, 8192], P(('layer', 'row'), 'col')
Inputs may be any that keep to these rules, and one draw needn't show every extreme that they name: pattern is symmetric and every diagonal block is kept. factor is zero below its diagonal and in every block that pattern does not keep. adjoint is zero in every block that pattern does not keep.
All inputs are finite; a program needn't handle non-finite values.
Results may differ from a plain program's by a relative error of at most 0.0046.
Values may be sent and summed in bfloat16 or wider, within the bound.
A program may use at most 64 MiB of HBM per device.

v0:
```python
import jax
import jax.numpy as jnp
from jax import lax
from jax.sharding import PartitionSpec as P

BLK = 128


def block_keep(pattern_f, row_first, row_count, col_first, col_count):
    blocks = pattern_f.shape[0]
    labels = jnp.arange(blocks, dtype=jnp.int32)
    rows = (row_first + jnp.arange(row_count, dtype=jnp.int32)) // BLK
    cols = (col_first + jnp.arange(col_count, dtype=jnp.int32)) // BLK
    pick_rows = (rows[:, None] == labels[None, :]).astype(jnp.float32)
    pick_cols = (labels[:, None] == cols[None, :]).astype(jnp.float32)
    half = jnp.dot(pick_rows, pattern_f, precision=lax.Precision.HIGHEST)
    return jnp.dot(half, pick_cols, precision=lax.Precision.HIGHEST)


def upper_weight(row_first, row_count, col_first, col_count):
    rows = row_first + jnp.arange(row_count, dtype=jnp.int32)
    cols = col_first + jnp.arange(col_count, dtype=jnp.int32)
    below = rows[:, None] < cols[None, :]
    equal = rows[:, None] == cols[None, :]
    return jnp.where(below, jnp.float32(1.0), jnp.where(equal, jnp.float32(0.5), jnp.float32(0.0)))


def per_device(factor, adjoint, pattern):
    row_index = lax.axis_index("row")
    col_index = lax.axis_index("col")
    layer_index = lax.axis_index("layer")
    pattern_f = pattern.astype(jnp.float32)
    adjoint_cols = lax.all_gather(adjoint, "row", axis=1, tiled=True)
    inner = lax.dot_general(
        lax.all_gather(factor, "col", axis=1, tiled=True),
        adjoint_cols,
        (((0,), (0,)), ((), ())),
        preferred_element_type=jnp.float32,
    )
    rows_here = inner.shape[0]
    cols_here = inner.shape[1]
    row_first = row_index * rows_here
    total = lax.psum(inner, "layer")
    col_first = col_index * cols_here
    scale = block_keep(pattern_f, row_first, rows_here, col_first, cols_here) * upper_weight(
        row_first, rows_here, col_first, cols_here
    )
    lowered = (total * scale).astype(jnp.bfloat16)
    partial_image = jnp.dot(
        lax.all_gather(factor, "col", axis=1, tiled=True),
        lowered,
        preferred_element_type=jnp.float32,
    )
    summed = lax.psum_scatter(partial_image, "row", scatter_dimension=0, tiled=True)
    out_rows = summed.shape[0]
    out_first = (layer_index * lax.axis_size("row") + row_index) * out_rows
    keep = block_keep(pattern_f, out_first, out_rows, col_index * cols_here, cols_here)
    return (summed * keep).astype(jnp.bfloat16)


def solution(mesh):
    placed = (P("layer", ("row", "col")), P("layer", ("col", "row")), P())
    return jax.shard_map(
        per_device,
        mesh=mesh,
        in_specs=placed,
        out_specs=P(("layer", "row"), "col"),
        check_vma=False,
    )
```

profile of v0, /device:TPU:1, one launch (start us, length us, event | category | flops | bytes accessed | tf_op | source)
XLA Modules:
  0.0 293.8 jit_solution(8576724985353950167)
XLA Ops:
  6.5 0.0 all-gather.5.cloned.1.call-start
  6.5 0.7 all-gather.5.cloned.1.call-update
  7.3 0.0 all-gather.3.cloned.1.call-start
  7.3 0.7 all-gather.3.cloned.1.call-update
  8.0 0.0 all-reduce.2.cloned.1.call-start
  8.1 41.1 %all-gather.5.cloned.1.call-done = bf16[2048,512]{1,0:T(8,128)(2,1)} async-done(((bf16[2048,128]{1,0:T(8,128)(2,1)}), bf16[2048,512]{1,0:T(8,128)(2,1)}) %all-gather.5.cloned.1.call-update) | async-done | bytes 2097168 | tf_op jit(solution)/shard_map/all_gather | solution.py:33
  49.2 70.2 %all-gather.3.cloned.1.call-done = bf16[2048,2048]{1,0:T(8,128)(2,1)} async-done(((bf16[2048,128]{1,0:T(8,128)(2,1)}), bf16[2048,2048]{1,0:T(8,128)(2,1)}) %all-gather.3.cloned.1.call-update) | async-done | bytes 8388624 | tf_op jit(solution)/shard_map/all_gather | solution.py:50
  119.4 10.5 %fusion.18 = f32[2048,512]{1,0:T(8,128)} fusion(bf16[2048,2048]{1,0:T(8,128)(2,1)} %all-gather.3.cloned.1.call-done, bf16[2048,512]{1,0:T(8,128)(2,1)} %all-gather.5.cloned.1.call-done), kind=kOutput, calls=%fused_computation.42 | convolution fusion | flops 4294967296 | bytes 14680064 | tf_op jit(solution)/shard_map/dot_general | solution.py:34
  129.9 0.0 copy-start
  129.9 0.0 all-reduce.2.cloned.1.call-update
  129.9 0.0 reduce-scatter.2.cloned.1.call-start
  130.0 0.6 copy-done
  130.6 0.7 fusion.1
  131.4 92.7 %all-reduce.2.cloned.1.call-done = f32[2048,512]{1,0:T(8,128)} async-done(((f32[2048,512]{1,0:T(8,128)}), f32[2048,512]{1,0:T(8,128)}) %all-reduce.2.cloned.1.call-update) | async-done | bytes 4194320 | tf_op jit(solution)/shard_map/psum | solution.py:43
  224.1 0.0 copy-start.1
  224.1 4.2 %multiply_convert_fusion = bf16[2048,512]{1,0:T(8,128)(2,1)S(1)} fusion(f32[2048,512]{1,0:T(8,128)} %all-reduce.2.cloned.1.call-done, f32[2048,64]{1,0:T(8,128)S(1)} %fusion.1, s32[512]{0:T(512)S(1)} %get-tuple-element.8, s32[2048]{0:T(1024)S(1)} %get-tuple-element.6, s32[512]{0:T(512)S(1)} %get-tuple-element.7), kind=kOutput, calls=%fused_computation | convolution fusion | flops 812679168 | bytes 6828032 | tf_op jit(solution)/shard_map/dot_general | solution.py:17
  228.3 0.4 copy-done.1
  228.7 6.2 %convolution_bitcast_fusion = f32[2048,512]{0,1:T(8,128)} fusion(bf16[2048,512]{1,0:T(8,128)(2,1)S(1)} %multiply_convert_fusion, bf16[2048,2048]{1,0:T(8,128)(2,1)S(1)} %copy-done.1), kind=kOutput, calls=%fused_computation.1 | convolution fusion | flops 4294967296 | bytes 14680064 | tf_op jit(solution)/shard_map/dot_general | solution.py:49
  234.9 0.0 reduce-scatter.2.cloned.1.call-update
  234.9 0.3 fusion.3
  235.3 49.1 %reduce-scatter.2.cloned.1.call-done = f32[512,512]{0,1:T(8,128)} async-done(((f32[2048,512]{0,1:T(8,128)}), f32[512,512]{0,1:T(8,128)}) %reduce-scatter.2.cloned.1.call-update) | async-done | bytes 1048592 | tf_op jit(solution)/shard_map/reduce_scatter | solution.py:54
  284.4 1.9 fusion
  286.3 1.0 copy.5
  (3 shorter events, 0.0 us)
Async XLA Ops:
  6.5 42.7 %all-gather.5.cloned.1.call-start = ((), (), s32[]{:S(2)}) async-start(), calls=%async_computation.2 | async-start | bytes 2621440 | tf_op jit(solution)/shard_map/all_gather | solution.py:33
  7.3 112.1 %all-gather.3.cloned.1.call-start = ((), (), s32[]{:S(2)}) async-start(), calls=%async_computation.1 | async-start | bytes 8912896 | tf_op jit(solution)/shard_map/all_gather | solution.py:50
  8.0 216.1 %all-reduce.2.cloned.1.call-start = ((), (), s32[]{:S(2)}) async-start(), calls=%async_computation.3 | async-start | bytes 8388608 | tf_op jit(solution)/shard_map/psum | solution.py:43
  129.9 0.8 copy-start
  129.9 154.5 %reduce-scatter.2.cloned.1.call-start = ((), (), s32[]{:S(2)}) async-start(), calls=%async_computation.4 | async-start | bytes 5242880 | tf_op jit(solution)/shard_map/reduce_scatter | solution.py:54
  224.1 4.6 %copy-start.1 = (bf16[2048,2048]{1,0:T(8,128)(2,1)S(1)}, bf16[2048,2048]{1,0:T(8,128)(2,1)}, u32[]{:S(2)}) copy-start(bf16[2048,2048]{1,0:T(8,128)(2,1)} %all-gather.3.cloned.1.call-done) | copy-start | bytes 25165828
Sparse Core Ops, SparseCore 0:
  9.2 39.9 all-gather.4
  50.9 68.3 all-gather.2
  130.0 93.9 all-reduce.1
  235.0 49.3 reduce-scatter.1
where the time goes:
time: 294 us
  waiting for transfers between devices  255 us (87%)
  matrix products  23.8 us (8%)
  between operations  13.2 us (4%)
    psum x1, waiting for transfers between devices, per_device(): total = lax.psum(inner, 'layer')  92.7 us
    all_gather x1, waiting for transfers between devices, per_device(): lax.all_gather(factor, 'col', axis=1, tiled=True)  70.2 us
    reduce_scatter x1, waiting for transfers between devices, per_device(): lax.psum_scatter(partial_image, 'row', scatter_dimension=0, tiled=True)  49.1 us
    all_gather x1, waiting for transfers between devices, per_device(): adjoint_cols = lax.all_gather(adjoint, 'row', axis=1, tiled=True)  41.1 us
    dot_general x1, matrix products, per_device(): lax.dot_general(lax.all_gather(factor, 'col', axis=1, tiled=True), adjoin...  10.5 us
    dot_general x1, matrix products, per_device(): jnp.dot(lax.all_gather(factor, 'col', axis=1, tiled=True), lowered, prefe...  6.17 us
    dot_general x2, matrix products, block_keep(): return jnp.dot(half, pick_cols, precision=lax.Precision.HIGHEST)  6.09 us
  transfers between devices with their start and end apart: 4, of which 4 were waited for; matrix products, arithmetic and copies ran while one was open for 0% of the time, Pallas kernels for 0%

commit v1 on v0

v1 whole, which is shorter than its diff:
```python
import functools

import jax
import jax.numpy as jnp
from jax import lax
from jax.experimental import pallas as pl
from jax.experimental.pallas import tpu as pltpu
from jax.sharding import PartitionSpec as P

BLK = 128
NR, NZ, NL = 4, 8, 4
ROWS = 2048
MESH = pl.DeviceIdType.MESH
F32 = jnp.float32
BF16 = jnp.bfloat16


def kernel(
    f_ref, a_ref, pat_ref, out_ref,
    fd, ad, at, acc, psend, pown, prec, lx, img, isend, irec,
    s_r, r_r, s_l, r_l, s_s, r_s, s_a, r_a, s_p, r_p, s_x, r_x, s_i, r_i,
):
    r, c, l = lax.axis_index("row"), lax.axis_index("col"), lax.axis_index("layer")
    z, k = c // 2, c % 2

    def at_z(d):
        return (r, lax.rem(z + d + NZ, NZ) * 2 + k, l)

    def at_y(d):
        return (lax.rem(r + d, NR), c, l)

    def at_x(d):
        return (r, c, lax.rem(l + d, NL))

    sibling = (r, z * 2 + 1 - k, l)
    partners = [at_z(1), at_z(-1), sibling]
    partners += [at_y(d) for d in (1, 2, 3)] + [at_x(d) for d in (1, 2, 3)]
    barrier = pltpu.get_barrier_semaphore()
    for p in partners:
        pl.semaphore_signal(barrier, inc=1, device_id=p, device_id_type=MESH)
    pl.semaphore_wait(barrier, len(partners))

    def zpos(d):
        return lax.rem(z + d + NZ, NZ)

    def remote(src, dst, ss, rs, dev):
        return pltpu.make_async_remote_copy(
            src_ref=src, dst_ref=dst, send_sem=ss, recv_sem=rs, device_id=dev, device_id_type=MESH
        )

    HALF = ROWS // 2

    def part(ref, h):
        return ref.at[pl.ds(h * HALF, HALF)]

    def f_src(d, h):
        return part(f_ref if d == 0 else fd.at[zpos(d), k], h)

    def ring_r(s, h):
        return remote(f_src(-s, h), part(fd.at[zpos(-s), k], h), s_r.at[s, h], r_r.at[s, h], at_z(1))

    def ring_l(s, h):
        return remote(f_src(s, h), part(fd.at[zpos(s), k], h), s_l.at[s, h], r_l.at[s, h], at_z(-1))

    def share(d, h):
        return remote(f_src(d, h), part(fd.at[zpos(d), k], h), s_s.at[d % NZ, h], r_s.at[d % NZ, h], sibling)

    def a_copy(d):
        return remote(a_ref, ad.at[r], s_a.at[d - 1], r_a.at[d - 1], at_y(d))

    started = []

    def go(copy):
        copy.start()
        started.append(copy)

    for h in range(2):
        go(ring_r(0, h))
        go(ring_l(0, h))
    for d in (2, 1, 3):
        go(a_copy(d))
    for h in range(2):
        go(share(0, h))

    def arrive_r(s, h):
        ring_r(s, h).wait_recv()
        if s < 2 or (s == 2 and h == 0):
            go(ring_r(s + 1, h))
        go(share(-(s + 1), h))

    def arrive_l(s, h):
        ring_l(s, h).wait_recv()
        if s < 2 or (s == 2 and h == 1):
            go(ring_l(s + 1, h))
        go(share(s + 1, h))

    fd[z, k] = f_ref[...]
    ad[r] = a_ref[...]
    for s in range(2):
        for h in range(2):
            arrive_r(s, h)
            arrive_l(s, h)

    for d in (1, 2, 3):
        a_copy(d).wait_recv()

    @pl.loop(0, NR * 16)
    def _(i):
        q, b = i // 16, i % 16
        at[pl.ds(pl.multiple_of(q * BLK, BLK), BLK), pl.ds(pl.multiple_of(b * BLK, BLK), BLK)] = (
            ad[q, pl.ds(pl.multiple_of(b * BLK, BLK), BLK), :].T
        )

    def p_copy(d, w):
        return remote(psend.at[lax.rem(l + d, NL), w], prec.at[d - 1, w], s_p.at[d - 1, w], r_p.at[d - 1, w], at_x(d))

    def x_copy(d, w):
        return remote(lx.at[w, l], lx.at[w, l], s_x.at[d - 1, w], r_x.at[d - 1, w], at_x(d))

    def first(lo, step, n):
        @pl.loop(0, n)
        def _(i):
            w = zpos(lo + step * i)
            res = jnp.dot(
                at[...], jnp.concatenate([fd[w, 0], fd[w, 1]], axis=1), preferred_element_type=F32
            )
            acc[...] = res.reshape(4, BLK, 256)
            psend[:, w] = res.astype(BF16).reshape(4, BLK, 256)
            pown[w] = acc[l]
            for d in (2, 1, 3):
                p_copy(d, w).start()

    def middle(lo, step, n):
        @pl.loop(0, n)
        def _(i):
            w = zpos(lo + step * i)
            for d in (1, 2, 3):
                p_copy(d, w).wait_recv()
            total = pown[w] + prec[0, w].astype(F32) + prec[1, w].astype(F32) + prec[2, w].astype(F32)
            jb = 4 * c + l
            for u in range(2):
                ib = 16 * r + 2 * w + u
                t = total[:, u * BLK : (u + 1) * BLK].T
                ii = ib * BLK + lax.broadcasted_iota(jnp.int32, (BLK, BLK), 0)
                jj = jb * BLK + lax.broadcasted_iota(jnp.int32, (BLK, BLK), 1)
                wt = jnp.where(ii < jj, 1.0, jnp.where(ii == jj, 0.5, 0.0)).astype(F32)
                kp = pat_ref[ib, jb].astype(F32)
                lx[w, l, pl.ds(u * BLK, BLK), :] = (kp * t * wt).astype(BF16)
            for d in (2, 1, 3):
                x_copy(d, w).start()

    def ready(lo, step, n):
        @pl.loop(0, n)
        def _(i):
            w = zpos(lo + step * i)
            for d in (1, 2, 3):
                x_copy(d, w).wait_recv()

    def wait_share(d):
        for h in range(2):
            share(d, h).wait_recv()

    for d in (0, 1, -1):
        wait_share(d)
    first(-1, 1, 3)
    for d in (2, -2):
        wait_share(d)
    first(-2, 4, 2)
    for h in range(2):
        arrive_r(2, h)
        arrive_l(2, h)
    middle(-1, 1, 3)
    middle(-2, 4, 2)
    wait_share(3)
    wait_share(-3)
    first(3, 2, 2)
    ring_r(3, 0).wait_recv()
    go(share(4, 0))
    ring_l(3, 1).wait_recv()
    go(share(4, 1))
    ready(-1, 1, 3)
    ready(-2, 4, 2)

    def product(rows, offs):
        fs = jnp.concatenate([fd[zpos(o), u, rows, :] for o in offs for u in range(2)], axis=1)
        ls = jnp.concatenate(
            [jnp.concatenate([lx[zpos(o), j] for j in range(4)], axis=1) for o in offs], axis=0
        )
        return jnp.dot(fs, ls, preferred_element_type=F32)

    RC = 256

    @pl.loop(0, ROWS // RC)
    def _(i):
        rows = pl.ds(pl.multiple_of(i * RC, RC), RC)
        img[rows, :] = product(rows, (-2, -1, 0, 1, 2))

    wait_share(4)
    first(4, 1, 1)
    middle(3, 2, 2)
    middle(4, 1, 1)
    ready(3, 2, 2)
    ready(4, 1, 1)

    def i_copy(d, h):
        return remote(
            isend.at[d - 1, pl.ds(h * RC, RC)], irec.at[d - 1, pl.ds(h * RC, RC)],
            s_i.at[d - 1, h], r_i.at[d - 1, h], at_y(d),
        )

    for d in (2, 1, 3, 0):
        for h in range(2):
            base = lax.rem(r + d, NR) * 512 + h * RC
            rows = pl.ds(pl.multiple_of(base, RC), RC)
            res = img[rows, :] + product(rows, (3, 4, 5))
            if d:
                isend[d - 1, pl.ds(h * RC, RC), :] = res.astype(BF16)
                go(i_copy(d, h))
            else:
                img[rows, :] = res

    for h in range(2):
        for d in (1, 2, 3):
            i_copy(d, h).wait_recv()
        for b in range(2):
            q = h * 2 + b
            here = pl.ds(q * BLK, BLK)
            base = r * 512 + q * BLK
            tot = img[pl.ds(pl.multiple_of(base, BLK), BLK), :]
            for d in range(3):
                tot = tot + irec[d, here, :].astype(F32)
            kb = 4 * (4 * l + r) + q
            for j in range(4):
                kp = pat_ref[kb, 4 * c + j].astype(F32)
                cols = slice(j * BLK, (j + 1) * BLK)
                out_ref[here, cols] = (tot[:, cols] * kp).astype(BF16)

    for copy in started:
        copy.wait_send()

    @pl.loop(0, NZ)
    def _(w):
        for d in (1, 2, 3):
            p_copy(d, w).wait_send()
            x_copy(d, w).wait_send()


def per_device(factor, adjoint, pattern):
    dma = pltpu.SemaphoreType.DMA
    vmem = pl.BlockSpec(memory_space=pltpu.VMEM)
    return pl.pallas_call(
        kernel,
        out_shape=jax.ShapeDtypeStruct((512, 512), BF16),
        in_specs=[vmem, vmem, pl.BlockSpec(memory_space=pltpu.SMEM)],
        out_specs=vmem,
        scratch_shapes=[
            pltpu.VMEM((NZ, 2, ROWS, BLK), BF16),
            pltpu.VMEM((NR, ROWS, BLK), BF16),
            pltpu.VMEM((512, ROWS), BF16),
            pltpu.VMEM((4, BLK, 256), F32),
            pltpu.VMEM((4, NZ, BLK, 256), BF16),
            pltpu.VMEM((NZ, BLK, 256), F32),
            pltpu.VMEM((3, NZ, BLK, 256), BF16),
            pltpu.VMEM((NZ, 4, 256, BLK), BF16),
            pltpu.VMEM((ROWS, 512), F32),
            pltpu.VMEM((3, 512, 512), BF16),
            pltpu.VMEM((3, 512, 512), BF16),
            dma((4, 2)), dma((4, 2)), dma((4, 2)), dma((4, 2)),
            dma((NZ, 2)), dma((NZ, 2)),
            dma((3,)), dma((3,)),
            dma((3, NZ)), dma((3, NZ)),
            dma((3, NZ)), dma((3, NZ)),
            dma((3, 2)), dma((3, 2)),
        ],
        compiler_params=pltpu.CompilerParams(
            collective_id=0, has_side_effects=True, vmem_limit_bytes=56 << 20
        ),
        cost_estimate=pl.CostEstimate(flops=1 << 33, bytes_accessed=2 << 20, transcendentals=0),
    )(factor, adjoint, pattern)


def solution(mesh):
    placed = (P("layer", ("row", "col")), P("layer", ("col", "row")), P())
    return jax.shard_map(
        per_device,
        mesh=mesh,
        in_specs=placed,
        out_specs=P(("layer", "row"), "col"),
        check_vma=False,
    )
```

time: 294 us -> 113 us (0.38)
  the two profiles are of different devices: /device:TPU:1 before, /device:TPU:168 now
where the time goes in v1:
time: 113 us
  Pallas kernels  111 us (98%)
  local copies, waits for them, and re-layouts  1.87 us (2%)
    pallas_call x1, Pallas kernels, per_device(): pl.pallas_call(kernel, out_shape=jax.ShapeDtypeStruct((512, 512), BF16),...  111 us

profile of v1, /device:TPU:168, one launch (start us, length us, event | category | flops | bytes accessed | tf_op | source)
XLA Modules:
  0.0 113.2 jit_solution(739378786892003273)
XLA Ops:
  0.0 111.3 %shard_map.37 = bf16[512,512]{1,0:T(8,128)(2,1)} custom-call(bf16[2048,128]{1,0:T(8,128)(2,1)} %f_ref.1, bf16[2048,128]{1,0:T(8,128)(2,1)} %a_ref.1, s32[64,64]{1,0:T(8,128)} %pat_ref.1), custom_call_target="tpu_custom_call" | custom-call | flops 8589934592 | bytes 2097152 | tf_op jit(solution)/shard_map/pallas_call | solution.py:251
  111.3 1.9 %copy.5 = bf16[512,512]{1,0:T(8,128)(2,1)} copy(bf16[512,512]{1,0:T(8,128)(2,1)} %shard_map.37) | data formatting | bytes 1048576

commit v2 on v1

--- a/solution.py
+++ b/solution.py
@@ -245,7 +245,7 @@
             x_copy(d, w).wait_send()
 
 
-def per_device(factor, adjoint, pattern):
+def dense_device(factor, adjoint, pattern):
     dma = pltpu.SemaphoreType.DMA
     vmem = pl.BlockSpec(memory_space=pltpu.VMEM)
     return pl.pallas_call(
@@ -279,6 +279,436 @@
     )(factor, adjoint, pattern)
 
 
+CF, CA, CI = 8, 10, 10
+GROUPS = ((-2, 5, 20), (3, 3, 12))
+
+
+def sparse_kernel(
+    f_ref, a_ref, pat_ref, out_ref,
+    ownf, fs, fd, asl, at, acc, psend, prec, lsl, lx, img, ib, isend, irec,
+    nxt, fenc, fdec, aenc, adec, penc, pdec, ienc, idec,
+    s_o, r_o, s_r, r_r, s_l, r_l, s_s, r_s, s_a, r_a, s_p, r_p, s_x, r_x, s_i, r_i,
+):
+    r, c, l = lax.axis_index("row"), lax.axis_index("col"), lax.axis_index("layer")
+    z, k = c // 2, c % 2
+
+    def zpos(d):
+        return lax.rem(z + d + NZ, NZ)
+
+    def at_z(d):
+        return (r, zpos(d) * 2 + k, l)
+
+    def at_y(d):
+        return (lax.rem(r + d + NR, NR), c, l)
+
+    def at_x(d):
+        return (r, c, lax.rem(l + d, NL))
+
+    sibling = (r, z * 2 + 1 - k, l)
+    partners = [at_z(1), at_z(-1), sibling]
+    partners += [at_y(d) for d in (1, 2, 3)] + [at_x(d) for d in (1, 2, 3)]
+    barrier = pltpu.get_barrier_semaphore()
+    for p in partners:
+        pl.semaphore_signal(barrier, inc=1, device_id=p, device_id_type=MESH)
+
+    def remote(src, dst, ss, rs, dev):
+        return pltpu.make_async_remote_copy(
+            src_ref=src, dst_ref=dst, send_sem=ss, recv_sem=rs, device_id=dev, device_id_type=MESH
+        )
+
+    started = []
+
+    def go(copy):
+        copy.start()
+        started.append(copy)
+
+    def kept(row, col):
+        return jnp.where(row <= col, pat_ref[row, col], 0)
+
+    def ranks(n, bit, dec, off, cap):
+        def body(b, cnt):
+            one = bit(b)
+            dec[off + b] = jnp.where(one > 0, jnp.minimum(cnt, cap - 1), -1)
+            return cnt + one
+
+        lax.fori_loop(0, n, body, jnp.int32(0))
+
+    def picks(n, bit, enc, off, cap):
+        nxt[n] = 0
+
+        def back(i, nx):
+            b = n - 1 - i
+            nx = jnp.where(bit(b) > 0, b, nx)
+            nxt[b] = nx
+            return nx
+
+        lax.fori_loop(0, n, back, jnp.int32(0))
+
+        def chain(t, p):
+            e = nxt[p]
+            enc[off + t] = e
+            return e + 1
+
+        lax.fori_loop(0, cap, chain, jnp.int32(0))
+
+    def f_bit(w):
+        return lambda b: kept(16 * l + b % 16, 16 * r + 2 * w + b // 16)
+
+    def a_bit(q):
+        return lambda b: kept(16 * l + b, 4 * c + q)
+
+    def p_bit(lo):
+        return lambda b: kept(16 * r + 2 * zpos(lo + b // 8) + (b // 4) % 2, 4 * c + b % 4)
+
+    def i_bit(q):
+        return lambda b: kept(16 * l + 4 * q + b // 4, 4 * c + b % 4)
+
+    def zero_or(dec, val):
+        return jnp.where(dec >= 0, val, jnp.zeros_like(val))
+
+    picks(16, a_bit(r), aenc, 0, CA)
+    picks(32, f_bit(z), fenc, 0, 2 * CF)
+    pl.semaphore_wait(barrier, len(partners))
+
+    go(remote(f_ref, ownf.at[k], s_o, r_o, sibling))
+    ownf[k] = f_ref[...]
+
+    @pl.loop(0, CA)
+    def _(t):
+        asl[0][t] = a_ref[aenc[t]].T
+
+    AH = CA // 2
+
+    def a_first(d, h):
+        sl = pl.ds(h * AH, AH)
+        return remote(asl[0].at[sl], asl[(-d) % 4].at[sl], s_a.at[d % 4, h], r_a.at[d % 4, h], at_y(d))
+
+    def a_second(d):
+        h = 0 if d == 1 else 1
+        sl = pl.ds(h * AH, AH)
+        return remote(asl[(-d) % 4].at[sl], asl[2].at[sl], s_a.at[2, h], r_a.at[2, h], at_y(d))
+
+    for h in range(2):
+        go(a_first(1, h))
+        go(a_first(-1, 1 - h))
+
+    own_col = remote(f_ref, ownf.at[k], s_o, r_o, sibling)
+    own_col.wait_recv()
+
+    @pl.loop(0, CF)
+    def _(t):
+        e = fenc[k * CF + t]
+        fs[0][k * CF + t] = ownf[e // 16, e % 16]
+
+    HF = CF // 2
+
+    def fslot(d, h):
+        return fs[d % NZ].at[pl.ds(k * CF + h * HF, HF)]
+
+    def ring_r(s, h):
+        return remote(fslot(-s, h), fslot(-s - 1, h), s_r.at[s, h], r_r.at[s, h], at_z(1))
+
+    def ring_l(s, h):
+        return remote(fslot(s, h), fslot(s + 1, h), s_l.at[s, h], r_l.at[s, h], at_z(-1))
+
+    def share(d, h):
+        return remote(fslot(d, h), fslot(d, h), s_s.at[d % NZ, h], r_s.at[d % NZ, h], sibling)
+
+    for h in range(2):
+        go(ring_r(0, h))
+        go(ring_l(0, h))
+
+    def arrive_r(s, h):
+        ring_r(s, h).wait_recv()
+        if s < 2 or (s == 2 and h == 0):
+            go(ring_r(s + 1, h))
+        go(share(-(s + 1), h))
+
+    def arrive_l(s, h):
+        ring_l(s, h).wait_recv()
+        if s < 2 or (s == 2 and h == 1):
+            go(ring_l(s + 1, h))
+        go(share(s + 1, h))
+
+    for u in range(2):
+        for b in range(16):
+            fd[z, u, pl.ds(b * BLK, BLK), :] = ownf[u, b]
+
+    for q in range(4):
+        ranks(16, a_bit(q), adec, q * 16, CA)
+
+    def f_ranks(d):
+        ranks(32, f_bit(zpos(d)), fdec, (d % NZ) * 32, 2 * CF)
+
+    def a_expand(e):
+        q = lax.rem(r + e, NR)
+
+        @pl.loop(0, 16)
+        def _(b):
+            dec = adec[q * 16 + b]
+            rows = pl.ds(pl.multiple_of(q * BLK, BLK), BLK)
+            cols = pl.ds(pl.multiple_of(b * BLK, BLK), BLK)
+            at[rows, cols] = zero_or(dec, asl[e][jnp.maximum(dec, 0)])
+
+    def f_expand(d):
+        w = zpos(d)
+        for h in range(2):
+            share(d, h).wait_recv()
+
+        @pl.loop(0, 32)
+        def _(b):
+            dec = fdec[(d % NZ) * 32 + b]
+            rows = pl.ds(pl.multiple_of((b % 16) * BLK, BLK), BLK)
+            fd[w, b // 16, rows, :] = zero_or(dec, fs[d % NZ][jnp.maximum(dec, 0)])
+
+    def first(g, d):
+        w = zpos(d)
+        lo = GROUPS[g][0]
+        res = jnp.dot(at[...], jnp.concatenate([fd[w, 0], fd[w, 1]], axis=1), preferred_element_type=F32)
+        for u in range(2):
+            for j in range(4):
+                acc[g][(d - lo) * 8 + u * 4 + j] = res[j * BLK : (j + 1) * BLK, u * BLK : (u + 1) * BLK]
+
+    def p_copy(g, d):
+        n = GROUPS[g][2] // 4
+        mine = pl.ds(lax.rem(l + d, NL) * n, n)
+        return remote(psend[g].at[mine], prec[g].at[d - 1], s_p.at[g, d - 1], r_p.at[g, d - 1], at_x(d))
+
+    def x_copy(g, d):
+        n = GROUPS[g][2] // 4
+        mine = lsl[g].at[pl.ds(l * n, n)]
+        return remote(mine, mine, s_x.at[g, d - 1], r_x.at[g, d - 1], at_x(d))
+
+    def p_tables(g):
+        lo, n, cap = GROUPS[g]
+        picks(n * 8, p_bit(lo), penc[g], 0, cap)
+        ranks(n * 8, p_bit(lo), pdec[g], 0, cap)
+
+    def p_send(g):
+        @pl.loop(0, GROUPS[g][2])
+        def _(t):
+            psend[g][t] = acc[g][penc[g][t]].astype(BF16)
+
+        for d in (2, 1, 3):
+            go(p_copy(g, d))
+
+    def middle(g):
+        lo, _, cap = GROUPS[g]
+        n = cap // 4
+        for d in (1, 2, 3):
+            p_copy(g, d).wait_recv()
+
+        @pl.loop(0, n)
+        def _(t):
+            e = penc[g][l * n + t]
+            tot = acc[g][e]
+            for d in range(3):
+                tot = tot + prec[g][d, t].astype(F32)
+            row = 16 * r + 2 * zpos(lo + e // 8) + (e // 4) % 2
+            col = 4 * c + e % 4
+            ii = row * BLK + lax.broadcasted_iota(jnp.int32, (BLK, BLK), 0)
+            jj = col * BLK + lax.broadcasted_iota(jnp.int32, (BLK, BLK), 1)
+            wt = jnp.where(ii < jj, 1.0, jnp.where(ii == jj, 0.5, 0.0)).astype(F32)
+            lsl[g][l * n + t] = (tot.T * wt).astype(BF16)
+
+        for d in (2, 1, 3):
+            go(x_copy(g, d))
+
+    def l_expand(g):
+        lo, n, _ = GROUPS[g]
+        for d in (1, 2, 3):
+            x_copy(g, d).wait_recv()
+
+        @pl.loop(0, n * 8)
+        def _(b):
+            dec = pdec[g][b]
+            rows = pl.ds(pl.multiple_of(((b // 4) % 2) * BLK, BLK), BLK)
+            lx[zpos(lo + b // 8), b % 4, rows, :] = zero_or(dec, lsl[g][jnp.maximum(dec, 0)])
+
+    for d in (1, -1, 2, -2):
+        f_ranks(d)
+    for h in range(2):
+        a_first(1, h).wait_recv()
+        a_first(-1, 1 - h).wait_recv()
+        if h == 0:
+            go(a_second(1))
+            go(a_second(-1))
+    a_expand(0)
+    a_expand(1)
+    a_expand(3)
+    for h in range(2):
+        arrive_r(0, h)
+        arrive_l(0, h)
+    f_expand(1)
+    f_expand(-1)
+    a_second(1).wait_recv()
+    a_second(-1).wait_recv()
+    a_expand(2)
+    for d in (0, 1, -1):
+        first(0, d)
+    p_tables(0)
+    for h in range(2):
+        arrive_r(1, h)
+        arrive_l(1, h)
+    for d in (2, -2):
+        f_expand(d)
+        first(0, d)
+    p_send(0)
+    for d in (3, -3, 4):
+        f_ranks(d)
+    p_tables(1)
+    for h in range(2):
+        arrive_r(2, h)
+        arrive_l(2, h)
+    for d in (3, -3):
+        f_expand(d)
+        first(1, d if d > 0 else d + NZ)
+    ring_r(3, 0).wait_recv()
+    go(share(4, 0))
+    ring_l(3, 1).wait_recv()
+    go(share(4, 1))
+    f_expand(4)
+    first(1, 4)
+    p_send(1)
+    middle(0)
+    for d in (1, 2, 3):
+        q = lax.rem(r + d, NR)
+        picks(16, i_bit(q), ienc, (d - 1) * CI, CI)
+    ranks(16, i_bit(r), idec, 0, CI)
+    middle(1)
+    l_expand(0)
+
+    def product(rows, offs):
+        fs_ = jnp.concatenate([fd[zpos(o), u, rows, :] for o in offs for u in range(2)], axis=1)
+        ls_ = jnp.concatenate(
+            [jnp.concatenate([lx[zpos(o), j] for j in range(4)], axis=1) for o in offs], axis=0
+        )
+        return jnp.dot(fs_, ls_, preferred_element_type=F32)
+
+    RC = 256
+
+    @pl.loop(0, ROWS // RC)
+    def _(i):
+        rows = pl.ds(pl.multiple_of(i * RC, RC), RC)
+        img[rows, :] = product(rows, (-2, -1, 0, 1, 2))
+
+    l_expand(1)
+
+    def i_copy(d):
+        return remote(isend.at[d - 1], irec[d - 1], s_i.at[d - 1], r_i.at[d - 1], at_y(d))
+
+    for d in (2, 1, 3, 0):
+        q = lax.rem(r + d, NR)
+        for h in range(2):
+            rows = pl.ds(pl.multiple_of(q * 512 + h * RC, RC), RC)
+            res = img[rows, :] + product(rows, (3, 4, 5))
+            for b in range(8):
+                i, j = b // 4, b % 4
+                ib[h * 8 + b] = res[i * BLK : (i + 1) * BLK, j * BLK : (j + 1) * BLK]
+        if d:
+            @pl.loop(0, CI)
+            def _(t):
+                isend[d - 1, t] = ib[ienc[(d - 1) * CI + t]].astype(BF16)
+
+            go(i_copy(d))
+
+    for d in (1, 2, 3):
+        i_copy(d).wait_recv()
+    for b in range(16):
+        dec = idec[b]
+        at_slot = jnp.maximum(dec, 0)
+        tot = ib[b]
+        for d in range(3):
+            tot = tot + irec[d][at_slot].astype(F32)
+        i, j = b // 4, b % 4
+        out_ref[pl.ds(i * BLK, BLK), j * BLK : (j + 1) * BLK] = zero_or(dec, tot).astype(BF16)
+
+    for copy in started:
+        copy.wait_send()
+
+
+def sparse_device(factor, adjoint, pattern):
+    dma, smem, scratch = pltpu.SemaphoreType.DMA, pltpu.SMEM, pltpu.VMEM
+    vmem = pl.BlockSpec(memory_space=pltpu.VMEM)
+    blocks = lambda *lead: scratch((*lead, BLK, BLK), BF16)
+    blocks32 = lambda *lead: scratch((*lead, BLK, BLK), F32)
+    ints = lambda n: smem((n,), jnp.int32)
+    caps = [g[2] for g in GROUPS]
+    sizes = [g[1] * 8 for g in GROUPS]
+    return pl.pallas_call(
+        sparse_kernel,
+        out_shape=jax.ShapeDtypeStruct((512, 512), BF16),
+        in_specs=[vmem, vmem, pl.BlockSpec(memory_space=pltpu.SMEM)],
+        out_specs=vmem,
+        scratch_shapes=[
+            blocks(2, 16),
+            [blocks(2 * CF) for _ in range(NZ)],
+            scratch((NZ, 2, ROWS, BLK), BF16),
+            [blocks(CA) for _ in range(NR)],
+            scratch((512, ROWS), BF16),
+            [blocks32(n) for n in sizes],
+            [blocks(n) for n in caps],
+            [blocks(3, n // 4) for n in caps],
+            [blocks(n) for n in caps],
+            scratch((NZ, 4, 256, BLK), BF16),
+            scratch((ROWS, 512), F32),
+            blocks32(16),
+            blocks(3, CI),
+            [blocks(CI) for _ in range(3)],
+            ints(72), ints(2 * CF), ints(NZ * 32), ints(CA), ints(64),
+            [ints(n) for n in caps], [ints(n) for n in sizes],
+            ints(3 * CI), ints(16),
+            dma, dma,
+            dma((4, 2)), dma((4, 2)), dma((4, 2)), dma((4, 2)),
+            dma((NZ, 2)), dma((NZ, 2)),
+            dma((4, 2)), dma((4, 2)),
+            dma((2, 3)), dma((2, 3)),
+            dma((2, 3)), dma((2, 3)),
+            dma((3,)), dma((3,)),
+        ],
+        compiler_params=pltpu.CompilerParams(
+            collective_id=1, has_side_effects=True, vmem_limit_bytes=56 << 20
+        ),
+        cost_estimate=pl.CostEstimate(flops=1 << 33, bytes_accessed=2 << 20, transcendentals=0),
+    )(factor.reshape(16, BLK, BLK), adjoint.reshape(16, BLK, BLK), pattern)
+
+
+def fits_kernel(pat_ref, out_ref):
+    def iota(shape, dim):
+        return lax.broadcasted_iota(jnp.int32, shape, dim)
+
+    def ones(cond):
+        return jnp.where(cond, 1.0, 0.0).astype(F32)
+
+    dot = functools.partial(jnp.dot, preferred_element_type=F32)
+    up = ones((iota((64, 64), 0) <= iota((64, 64), 1)) & (pat_ref[...] > 0))
+    quad = ones(iota((64, 16), 0) // 4 == iota((64, 16), 1))
+    pair = ones(iota((64, 32), 0) // 2 == iota((64, 32), 1))
+    pair_t = ones(iota((32, 64), 1) // 2 == iota((32, 64), 0))
+    quad_t = ones(iota((16, 64), 1) // 4 == iota((16, 64), 0))
+    wide_t = ones(iota((8, 64), 1) // 16 == iota((8, 64), 0))
+    cols = dot(wide_t, up)
+    good = (jnp.max(cols) <= CA) & (jnp.max(dot(cols, pair)) <= 2 * CF)
+    good = good & (jnp.max(dot(dot(quad_t, up), quad)) <= CI)
+    count = dot(dot(pair_t, up), quad)
+    a, b = iota((32, 32), 0), iota((32, 32), 1)
+    here = iota((32, 16), 0) % 8 == iota((32, 16), 1) // 2
+    for lo, n, cap in GROUPS:
+        window = ones((a // 8 == b // 8) & ((b % 8 - a % 8 - lo + 16) % 8 < n))
+        good = good & (jnp.max(jnp.where(here, dot(window, count), 0.0)) <= cap)
+    out_ref[0] = jnp.where(good, 1, 0)
+
+
+def per_device(factor, adjoint, pattern):
+    fits = pl.pallas_call(
+        fits_kernel,
+        out_shape=jax.ShapeDtypeStruct((1,), jnp.int32),
+        in_specs=[pl.BlockSpec(memory_space=pltpu.VMEM)],
+        out_specs=pl.BlockSpec(memory_space=pltpu.SMEM),
+    )(pattern)
+    return lax.cond(fits[0] > 0, sparse_device, dense_device, factor, adjoint, pattern)
+
+
 def solution(mesh):
     placed = (P("layer", ("row", "col")), P("layer", ("col", "row")), P())
     return jax.shard_map(

time: 113 us -> 87.4 us (0.77)
  the two profiles are of different devices: /device:TPU:168 before, /device:TPU:1 now
where the time goes in v2:
time: 87.4 us; the launch traced here: 87.3 us
  Pallas kernels  85.6 us (98%)
    pallas_call x1, Pallas kernels, sparse_device(): pl.pallas_call(sparse_kernel, out_shape=jax.ShapeDtypeStruct((512, 512),...  83.7 us
    pallas_call x1, Pallas kernels, per_device(): pl.pallas_call(fits_kernel, out_shape=jax.ShapeDtypeStruct((1,), jnp.int3...  1.84 us

profile of v2, /device:TPU:1, one launch (start us, length us, event | category | flops | bytes accessed | tf_op | source)
XLA Modules:
  0.0 87.3 jit_solution(14699992640631519752)
XLA Ops:
  0.0 0.0 copy-start
  0.0 1.8 %shard_map.43 = s32[1]{0:T(128)} custom-call(s32[64,64]{1,0:T(8,128)} %pat_ref.1), custom_call_target="tpu_custom_call" | custom-call | tf_op jit(solution)/shard_map/pallas_call | solution.py:703
  2.5 0.0 copy-done
  2.5 83.9 %conditional.1 = (bf16[512,512]{1,0:T(8,128)(2,1)S(1)}) conditional(s32[]{:T(128)} %bitcast.2, (bf16[2048,128]{1,0:T(8,128)(2,1)}, bf16[2048,128]{1,0:T(8,128)(2,1)}, s32[64,64]{1,0:T(8,128)S(1)}) %tuple.16, (bf16[2048,128]{1,0:T(8,128)(2,1)}, bf16[2048,128]{1,0:T(8,128)(2,1)}, s32[64,64]{1,0:T(8,128)S(1)}) %tuple.17), branch_computations={%region_0.0_spmd, %region_1.0_spmd} | conditional | flops 8589934592 | bytes 2097160 | solution.py:709
  2.7 83.7 %branch_1_fun.1 = bf16[512,512]{1,0:T(8,128)(2,1)S(1)} custom-call(bf16[16,128,128]{2,1,0:T(8,128)(2,1)} %bitcast.3, bf16[16,128,128]{2,1,0:T(8,128)(2,1)} %bitcast.4, s32[64,64]{1,0:T(8,128)S(1)} %get-tuple-element.25.pat_ref), custom_call_target="tpu_custom_call" | custom-call | flops 8589934592 | bytes 2097152 | tf_op jit(solution)/shard_map/cond/branch_1_fun/pallas_call | solution.py:638
  86.5 0.8 copy.13
Async XLA Ops:
  0.0 2.5 %copy-start = (s32[64,64]{1,0:T(8,128)S(1)}, s32[64,64]{1,0:T(8,128)}, u32[]{:S(2)}) copy-start(s32[64,64]{1,0:T(8,128)} %pat_ref.1) | copy-start | bytes 49156

commit v3 on v2

--- a/solution.py
+++ b/solution.py
@@ -245,7 +245,7 @@
             x_copy(d, w).wait_send()
 
 
-def dense_device(factor, adjoint, pattern):
+def dense_device(factor, adjoint, pattern, table):
     dma = pltpu.SemaphoreType.DMA
     vmem = pl.BlockSpec(memory_space=pltpu.VMEM)
     return pl.pallas_call(
@@ -279,16 +279,19 @@
     )(factor, adjoint, pattern)
 
 
-CF, CA, CI = 8, 10, 10
-GROUPS = ((-2, 5, 20), (3, 3, 12))
+SPANS = ((-2, 5), (3, 3))
+TIERS = ((6, 8, 8, 16, 12), (8, 12, 12, 20, 16))
 
 
 def sparse_kernel(
-    f_ref, a_ref, pat_ref, out_ref,
-    ownf, fs, fd, asl, at, acc, psend, prec, lsl, lx, img, ib, isend, irec,
-    nxt, fenc, fdec, aenc, adec, penc, pdec, ienc, idec,
+    caps, f_ref, a_ref, tab_ref, out_ref,
+    ownf, fs, fd, asl, at, acc, psend, prec, lsl, lx, img, ib, isend, relay, irec,
+    nxt, fenc, aenc, penc, ienc,
     s_o, r_o, s_r, r_r, s_l, r_l, s_s, r_s, s_a, r_a, s_p, r_p, s_x, r_x, s_i, r_i,
 ):
+    CF, CA, CI, *widths = caps
+    GROUPS = [(*span, width) for span, width in zip(SPANS, widths)]
+    HF = CF // 2
     r, c, l = lax.axis_index("row"), lax.axis_index("col"), lax.axis_index("layer")
     z, k = c // 2, c % 2
 
@@ -322,16 +325,19 @@
         copy.start()
         started.append(copy)
 
+    nothing = jnp.zeros((BLK, BLK), BF16)
+    for d in range(1, NZ):
+        fs[d][2 * CF] = nothing
+    for q in range(NR):
+        asl[q][CA] = nothing
+    for g in range(2):
+        lsl[g][GROUPS[g][2]] = nothing
+
+    def field(row, col, shift, mask):
+        return lax.shift_right_logical(tab_ref[row, col], shift) & mask
+
     def kept(row, col):
-        return jnp.where(row <= col, pat_ref[row, col], 0)
-
-    def ranks(n, bit, dec, off, cap):
-        def body(b, cnt):
-            one = bit(b)
-            dec[off + b] = jnp.where(one > 0, jnp.minimum(cnt, cap - 1), -1)
-            return cnt + one
-
-        lax.fori_loop(0, n, body, jnp.int32(0))
+        return field(row, col, 21, 1)
 
     def picks(n, bit, enc, off, cap):
         nxt[n] = 0
@@ -351,27 +357,62 @@
 
         lax.fori_loop(0, cap, chain, jnp.int32(0))
 
-    def f_bit(w):
-        return lambda b: kept(16 * l + b % 16, 16 * r + 2 * w + b // 16)
-
-    def a_bit(q):
-        return lambda b: kept(16 * l + b, 4 * c + q)
-
-    def p_bit(lo):
-        return lambda b: kept(16 * r + 2 * zpos(lo + b // 8) + (b // 4) % 2, 4 * c + b % 4)
-
-    def i_bit(q):
-        return lambda b: kept(16 * l + 4 * q + b // 4, 4 * c + b % 4)
-
-    def zero_or(dec, val):
-        return jnp.where(dec >= 0, val, jnp.zeros_like(val))
-
-    picks(16, a_bit(r), aenc, 0, CA)
-    picks(32, f_bit(z), fenc, 0, 2 * CF)
+    def f_dec(d, b):
+        return field(16 * l + b % 16, 16 * r + 2 * zpos(d) + b // 16, 0, 31)
+
+    def p_dec(i, j):
+        return field(16 * r + i, 4 * c + j, 10, 63)
+
+    def p_tables():
+        nxt[64] = 0
+        nxt[64 + 72] = 0
+
+        def back(t, carry):
+            b = 63 - t
+            i, j = b // 4, b % 4
+            near = lax.rem(i // 2 - z - SPANS[0][0] + NZ, NZ) < SPANS[0][1]
+            one = kept(16 * r + i, 4 * c + j) > 0
+            n0 = jnp.where(one & near, b, carry[0])
+            n1 = jnp.where(one & jnp.logical_not(near), b, carry[1])
+            nxt[b] = n0
+            nxt[72 + b] = n1
+            return n0, n1
+
+        lax.fori_loop(0, 64, back, (jnp.int32(0), jnp.int32(0)))
+        for g in range(2):
+            def chain(t, p, g=g):
+                e = nxt[72 * g + p]
+                penc[g][t] = e
+                return e + 1
+
+            lax.fori_loop(0, GROUPS[g][2], chain, jnp.int32(0))
+
     pl.semaphore_wait(barrier, len(partners))
 
-    go(remote(f_ref, ownf.at[k], s_o, r_o, sibling))
-    ownf[k] = f_ref[...]
+    own_col = remote(f_ref, ownf.at[k], s_o, r_o, sibling)
+    go(own_col)
+    picks(16, lambda b: kept(16 * l + b, 16 * r + 2 * z + k), fenc, 0, HF)
+
+    @pl.loop(0, HF)
+    def _(t):
+        fs[0][k * CF + t] = f_ref[fenc[t]]
+
+    def fslot(d, h):
+        return fs[d % NZ].at[pl.ds(k * CF + h * HF, HF)]
+
+    def ring_r(s, h):
+        return remote(fslot(-s, h), fslot(-s - 1, h), s_r.at[s, h], r_r.at[s, h], at_z(1))
+
+    def ring_l(s, h):
+        return remote(fslot(s, h), fslot(s + 1, h), s_l.at[s, h], r_l.at[s, h], at_z(-1))
+
+    def share(d, h):
+        return remote(fslot(d, h), fslot(d, h), s_s.at[d % NZ, h], r_s.at[d % NZ, h], sibling)
+
+    go(ring_r(0, 0))
+    go(ring_l(0, 0))
+
+    picks(16, lambda b: kept(16 * l + b, 4 * c + r), aenc, 0, CA)
 
     @pl.loop(0, CA)
     def _(t):
@@ -392,31 +433,23 @@
         go(a_first(1, h))
         go(a_first(-1, 1 - h))
 
-    own_col = remote(f_ref, ownf.at[k], s_o, r_o, sibling)
+    over = lambda b: jnp.where(f_dec(0, b) % CF >= HF, 1, 0)
+    picks(32, over, fenc, HF, 2 * HF)
+    ownf[k] = f_ref[...]
     own_col.wait_recv()
 
-    @pl.loop(0, CF)
+    @pl.loop(0, HF)
     def _(t):
-        e = fenc[k * CF + t]
-        fs[0][k * CF + t] = ownf[e // 16, e % 16]
-
-    HF = CF // 2
-
-    def fslot(d, h):
-        return fs[d % NZ].at[pl.ds(k * CF + h * HF, HF)]
-
-    def ring_r(s, h):
-        return remote(fslot(-s, h), fslot(-s - 1, h), s_r.at[s, h], r_r.at[s, h], at_z(1))
-
-    def ring_l(s, h):
-        return remote(fslot(s, h), fslot(s + 1, h), s_l.at[s, h], r_l.at[s, h], at_z(-1))
-
-    def share(d, h):
-        return remote(fslot(d, h), fslot(d, h), s_s.at[d % NZ, h], r_s.at[d % NZ, h], sibling)
-
-    for h in range(2):
-        go(ring_r(0, h))
-        go(ring_l(0, h))
+        e = fenc[HF + k * HF + t]
+        fs[0][k * CF + HF + t] = ownf[e // 16, e % 16]
+
+    go(ring_r(0, 1))
+    go(ring_l(0, 1))
+
+    p_tables()
+    for d in (1, 2, 3):
+        q = lax.rem(r + d, NR)
+        picks(16, lambda b: kept(16 * l + 4 * q + b // 4, 4 * c + b % 4), ienc, (d - 1) * CI, CI)
 
     def arrive_r(s, h):
         ring_r(s, h).wait_recv()
@@ -434,40 +467,33 @@
         for b in range(16):
             fd[z, u, pl.ds(b * BLK, BLK), :] = ownf[u, b]
 
-    for q in range(4):
-        ranks(16, a_bit(q), adec, q * 16, CA)
-
-    def f_ranks(d):
-        ranks(32, f_bit(zpos(d)), fdec, (d % NZ) * 32, 2 * CF)
-
     def a_expand(e):
         q = lax.rem(r + e, NR)
 
-        @pl.loop(0, 16)
+        @pl.loop(0, 16, unroll=4)
         def _(b):
-            dec = adec[q * 16 + b]
+            dec = field(16 * l + b, 4 * c + q, 5, 31)
             rows = pl.ds(pl.multiple_of(q * BLK, BLK), BLK)
             cols = pl.ds(pl.multiple_of(b * BLK, BLK), BLK)
-            at[rows, cols] = zero_or(dec, asl[e][jnp.maximum(dec, 0)])
+            at[rows, cols] = asl[e][dec]
 
     def f_expand(d):
         w = zpos(d)
         for h in range(2):
             share(d, h).wait_recv()
 
-        @pl.loop(0, 32)
+        @pl.loop(0, 32, unroll=4)
         def _(b):
-            dec = fdec[(d % NZ) * 32 + b]
+            dec = f_dec(d, b)
             rows = pl.ds(pl.multiple_of((b % 16) * BLK, BLK), BLK)
-            fd[w, b // 16, rows, :] = zero_or(dec, fs[d % NZ][jnp.maximum(dec, 0)])
+            fd[w, b // 16, rows, :] = fs[d % NZ][dec]
 
     def first(g, d):
         w = zpos(d)
-        lo = GROUPS[g][0]
         res = jnp.dot(at[...], jnp.concatenate([fd[w, 0], fd[w, 1]], axis=1), preferred_element_type=F32)
         for u in range(2):
             for j in range(4):
-                acc[g][(d - lo) * 8 + u * 4 + j] = res[j * BLK : (j + 1) * BLK, u * BLK : (u + 1) * BLK]
+                acc[w * 8 + u * 4 + j] = res[j * BLK : (j + 1) * BLK, u * BLK : (u + 1) * BLK]
 
     def p_copy(g, d):
         n = GROUPS[g][2] // 4
@@ -479,15 +505,10 @@
         mine = lsl[g].at[pl.ds(l * n, n)]
         return remote(mine, mine, s_x.at[g, d - 1], r_x.at[g, d - 1], at_x(d))
 
-    def p_tables(g):
-        lo, n, cap = GROUPS[g]
-        picks(n * 8, p_bit(lo), penc[g], 0, cap)
-        ranks(n * 8, p_bit(lo), pdec[g], 0, cap)
-
     def p_send(g):
         @pl.loop(0, GROUPS[g][2])
         def _(t):
-            psend[g][t] = acc[g][penc[g][t]].astype(BF16)
+            psend[g][t] = acc[penc[g][t]].astype(BF16)
 
         for d in (2, 1, 3):
             go(p_copy(g, d))
@@ -501,10 +522,10 @@
         @pl.loop(0, n)
         def _(t):
             e = penc[g][l * n + t]
-            tot = acc[g][e]
+            tot = acc[e]
             for d in range(3):
                 tot = tot + prec[g][d, t].astype(F32)
-            row = 16 * r + 2 * zpos(lo + e // 8) + (e // 4) % 2
+            row = 16 * r + e // 4
             col = 4 * c + e % 4
             ii = row * BLK + lax.broadcasted_iota(jnp.int32, (BLK, BLK), 0)
             jj = col * BLK + lax.broadcasted_iota(jnp.int32, (BLK, BLK), 1)
@@ -519,44 +540,40 @@
         for d in (1, 2, 3):
             x_copy(g, d).wait_recv()
 
-        @pl.loop(0, n * 8)
+        @pl.loop(0, n * 8, unroll=4)
         def _(b):
-            dec = pdec[g][b]
-            rows = pl.ds(pl.multiple_of(((b // 4) % 2) * BLK, BLK), BLK)
-            lx[zpos(lo + b // 8), b % 4, rows, :] = zero_or(dec, lsl[g][jnp.maximum(dec, 0)])
-
-    for d in (1, -1, 2, -2):
-        f_ranks(d)
-    for h in range(2):
-        a_first(1, h).wait_recv()
-        a_first(-1, 1 - h).wait_recv()
-        if h == 0:
-            go(a_second(1))
-            go(a_second(-1))
+            w, u, j = zpos(lo + b // 8), (b // 4) % 2, b % 4
+            dec = p_dec(2 * w + u, j)
+            lx[w, j, pl.ds(pl.multiple_of(u * BLK, BLK), BLK), :] = lsl[g][dec]
+
     a_expand(0)
+    a_first(1, 0).wait_recv()
+    a_first(-1, 1).wait_recv()
+    go(a_second(1))
+    go(a_second(-1))
+    arrive_r(0, 0)
+    arrive_l(0, 0)
+    a_first(1, 1).wait_recv()
+    a_first(-1, 0).wait_recv()
     a_expand(1)
     a_expand(3)
-    for h in range(2):
-        arrive_r(0, h)
-        arrive_l(0, h)
+    arrive_r(0, 1)
+    arrive_l(0, 1)
     f_expand(1)
     f_expand(-1)
     a_second(1).wait_recv()
     a_second(-1).wait_recv()
     a_expand(2)
+    arrive_r(1, 0)
+    arrive_l(1, 0)
     for d in (0, 1, -1):
         first(0, d)
-    p_tables(0)
-    for h in range(2):
-        arrive_r(1, h)
-        arrive_l(1, h)
+    arrive_r(1, 1)
+    arrive_l(1, 1)
     for d in (2, -2):
         f_expand(d)
         first(0, d)
     p_send(0)
-    for d in (3, -3, 4):
-        f_ranks(d)
-    p_tables(1)
     for h in range(2):
         arrive_r(2, h)
         arrive_l(2, h)
@@ -571,10 +588,6 @@
     first(1, 4)
     p_send(1)
     middle(0)
-    for d in (1, 2, 3):
-        q = lax.rem(r + d, NR)
-        picks(16, i_bit(q), ienc, (d - 1) * CI, CI)
-    ranks(16, i_bit(r), idec, 0, CI)
     middle(1)
     l_expand(0)
 
@@ -585,128 +598,173 @@
         )
         return jnp.dot(fs_, ls_, preferred_element_type=F32)
 
-    RC = 256
-
-    @pl.loop(0, ROWS // RC)
+    @pl.loop(0, ROWS // 512)
     def _(i):
-        rows = pl.ds(pl.multiple_of(i * RC, RC), RC)
+        rows = pl.ds(pl.multiple_of(i * 512, 512), 512)
         img[rows, :] = product(rows, (-2, -1, 0, 1, 2))
 
     l_expand(1)
 
-    def i_copy(d):
-        return remote(isend.at[d - 1], irec[d - 1], s_i.at[d - 1], r_i.at[d - 1], at_y(d))
+    HI = CI // 2
+
+    def i_relay(d):
+        half = pl.ds(0 if d == 1 else HI, HI)
+        return remote(isend.at[1, half], relay[d].at[...], s_i.at[d - 1, 2], r_i.at[d - 1, 2], at_y(d))
+
+    def i_copy(d, h):
+        half = pl.ds(h * HI, HI)
+        return remote(isend.at[d - 1, half], irec[d].at[half], s_i.at[d - 1, h], r_i.at[d - 1, h], at_y(d))
+
+    def i_pack(d, h, add):
+        @pl.loop(0, HI)
+        def _(t):
+            val = ib[d, ienc[(d - 1) * CI + h * HI + t]]
+            if add:
+                val = val + relay[d][t].astype(F32)
+            isend[d - 1, h * HI + t] = val.astype(BF16)
 
     for d in (2, 1, 3, 0):
         q = lax.rem(r + d, NR)
+        rows = pl.ds(pl.multiple_of(q * 512, 512), 512)
+        res = img[rows, :] + product(rows, (3, 4, 5))
+        for b in range(16):
+            i, j = b // 4, b % 4
+            ib[d, b] = res[i * BLK : (i + 1) * BLK, j * BLK : (j + 1) * BLK]
+        if d == 2:
+            i_pack(2, 0, False)
+            go(i_relay(1))
+            i_pack(2, 1, False)
+            go(i_relay(3))
+        elif d:
+            h = 1 if d == 1 else 0
+            i_pack(d, h, False)
+            go(i_copy(d, h))
+
+    for d in (1, 3):
+        h = 0 if d == 1 else 1
+        i_relay(d).wait_recv()
+        i_pack(d, h, True)
+        go(i_copy(d, h))
+    for d in (1, 3):
         for h in range(2):
-            rows = pl.ds(pl.multiple_of(q * 512 + h * RC, RC), RC)
-            res = img[rows, :] + product(rows, (3, 4, 5))
-            for b in range(8):
-                i, j = b // 4, b % 4
-                ib[h * 8 + b] = res[i * BLK : (i + 1) * BLK, j * BLK : (j + 1) * BLK]
-        if d:
-            @pl.loop(0, CI)
-            def _(t):
-                isend[d - 1, t] = ib[ienc[(d - 1) * CI + t]].astype(BF16)
-
-            go(i_copy(d))
-
-    for d in (1, 2, 3):
-        i_copy(d).wait_recv()
+            i_copy(d, h).wait_recv()
     for b in range(16):
-        dec = idec[b]
-        at_slot = jnp.maximum(dec, 0)
-        tot = ib[b]
-        for d in range(3):
+        dec = field(16 * l + 4 * r + b // 4, 4 * c + b % 4, 16, 31)
+        at_slot = jnp.minimum(dec, CI - 1)
+        tot = ib[0, b]
+        for d in (1, 3):
             tot = tot + irec[d][at_slot].astype(F32)
         i, j = b // 4, b % 4
-        out_ref[pl.ds(i * BLK, BLK), j * BLK : (j + 1) * BLK] = zero_or(dec, tot).astype(BF16)
+        out_ref[pl.ds(i * BLK, BLK), j * BLK : (j + 1) * BLK] = jnp.where(dec < CI, tot, 0.0).astype(BF16)
 
     for copy in started:
         copy.wait_send()
 
 
-def sparse_device(factor, adjoint, pattern):
+def sparse_device(tier, factor, adjoint, pattern, table):
+    CF, CA, CI, *caps = TIERS[tier]
     dma, smem, scratch = pltpu.SemaphoreType.DMA, pltpu.SMEM, pltpu.VMEM
     vmem = pl.BlockSpec(memory_space=pltpu.VMEM)
     blocks = lambda *lead: scratch((*lead, BLK, BLK), BF16)
     blocks32 = lambda *lead: scratch((*lead, BLK, BLK), F32)
     ints = lambda n: smem((n,), jnp.int32)
-    caps = [g[2] for g in GROUPS]
-    sizes = [g[1] * 8 for g in GROUPS]
     return pl.pallas_call(
-        sparse_kernel,
+        functools.partial(sparse_kernel, TIERS[tier]),
         out_shape=jax.ShapeDtypeStruct((512, 512), BF16),
         in_specs=[vmem, vmem, pl.BlockSpec(memory_space=pltpu.SMEM)],
         out_specs=vmem,
         scratch_shapes=[
             blocks(2, 16),
-            [blocks(2 * CF) for _ in range(NZ)],
+            [blocks(2 * CF + 1) for _ in range(NZ)],
             scratch((NZ, 2, ROWS, BLK), BF16),
-            [blocks(CA) for _ in range(NR)],
+            [blocks(CA + 1) for _ in range(NR)],
             scratch((512, ROWS), BF16),
-            [blocks32(n) for n in sizes],
+            blocks32(64),
             [blocks(n) for n in caps],
             [blocks(3, n // 4) for n in caps],
-            [blocks(n) for n in caps],
+            [blocks(n + 1) for n in caps],
             scratch((NZ, 4, 256, BLK), BF16),
             scratch((ROWS, 512), F32),
-            blocks32(16),
+            blocks32(4, 16),
             blocks(3, CI),
-            [blocks(CI) for _ in range(3)],
-            ints(72), ints(2 * CF), ints(NZ * 32), ints(CA), ints(64),
-            [ints(n) for n in caps], [ints(n) for n in sizes],
-            ints(3 * CI), ints(16),
+            [blocks(CI // 2) for _ in range(4)],
+            [blocks(CI) for _ in range(4)],
+            ints(144), ints(3 * CF), ints(CA), [ints(n) for n in caps], ints(3 * CI),
             dma, dma,
             dma((4, 2)), dma((4, 2)), dma((4, 2)), dma((4, 2)),
             dma((NZ, 2)), dma((NZ, 2)),
             dma((4, 2)), dma((4, 2)),
             dma((2, 3)), dma((2, 3)),
             dma((2, 3)), dma((2, 3)),
-            dma((3,)), dma((3,)),
+            dma((3, 3)), dma((3, 3)),
         ],
         compiler_params=pltpu.CompilerParams(
-            collective_id=1, has_side_effects=True, vmem_limit_bytes=56 << 20
+            collective_id=1 + tier, has_side_effects=True, vmem_limit_bytes=56 << 20
         ),
         cost_estimate=pl.CostEstimate(flops=1 << 33, bytes_accessed=2 << 20, transcendentals=0),
-    )(factor.reshape(16, BLK, BLK), adjoint.reshape(16, BLK, BLK), pattern)
-
-
-def fits_kernel(pat_ref, out_ref):
-    def iota(shape, dim):
-        return lax.broadcasted_iota(jnp.int32, shape, dim)
+    )(factor.reshape(16, BLK, BLK), adjoint.reshape(16, BLK, BLK), table)
+
+
+def plan_kernel(pat_ref, tier_ref, tab_ref):
+    row = lax.broadcasted_iota(jnp.int32, (64, 64), 0)
+    col = lax.broadcasted_iota(jnp.int32, (64, 64), 1)
 
     def ones(cond):
         return jnp.where(cond, 1.0, 0.0).astype(F32)
 
-    dot = functools.partial(jnp.dot, preferred_element_type=F32)
-    up = ones((iota((64, 64), 0) <= iota((64, 64), 1)) & (pat_ref[...] > 0))
-    quad = ones(iota((64, 16), 0) // 4 == iota((64, 16), 1))
-    pair = ones(iota((64, 32), 0) // 2 == iota((64, 32), 1))
-    pair_t = ones(iota((32, 64), 1) // 2 == iota((32, 64), 0))
-    quad_t = ones(iota((16, 64), 1) // 4 == iota((16, 64), 0))
-    wide_t = ones(iota((8, 64), 1) // 16 == iota((8, 64), 0))
-    cols = dot(wide_t, up)
-    good = (jnp.max(cols) <= CA) & (jnp.max(dot(cols, pair)) <= 2 * CF)
-    good = good & (jnp.max(dot(dot(quad_t, up), quad)) <= CI)
-    count = dot(dot(pair_t, up), quad)
-    a, b = iota((32, 32), 0), iota((32, 32), 1)
-    here = iota((32, 16), 0) % 8 == iota((32, 16), 1) // 2
-    for lo, n, cap in GROUPS:
-        window = ones((a // 8 == b // 8) & ((b % 8 - a % 8 - lo + 16) % 8 < n))
-        good = good & (jnp.max(jnp.where(here, dot(window, count), 0.0)) <= cap)
-    out_ref[0] = jnp.where(good, 1, 0)
+    def dot(x, y):
+        return jnp.dot(x.astype(BF16), y.astype(BF16), preferred_element_type=F32)
+
+    before16 = ones((row // 16 == col // 16) & (col < row))
+    same16 = ones(row // 16 == col // 16)
+    before4 = ones((row // 4 == col // 4) & (col < row))
+    quad = ones(row // 4 == col // 4)
+    ahead4 = ones((row // 4 == col // 4) & (row < col))
+    to_odd = ones((row + 1 == col) & (col % 2 == 1))
+    up = ones((row <= col) & (pat_ref[...] > 0))
+    rank = dot(before16, up)
+    in_quad = dot(up, ahead4)
+    i_rank = dot(before4, dot(up, quad)) + in_quad
+    p_rank, p_cap = jnp.zeros((64, 64), F32), []
+    near = []
+    for lo, n in SPANS:
+        member = ((row % 16) // 2 - col // 8 - lo + 16) % 8 < n
+        part = up * ones(member)
+        p_rank = jnp.where(member, dot(before16, dot(part, quad)) + dot(part, ahead4), p_rank)
+        near.append(member)
+    tier = len(TIERS)
+    table = None
+    for t in range(len(TIERS) - 1, -1, -1):
+        CF, CA, CI, *widths = TIERS[t]
+        HF = CF // 2
+        width = jnp.where(near[0], float(widths[0]), float(widths[1])).astype(F32)
+        late = up * ones(rank >= HF)
+        more = dot(before16, late) + dot(same16, dot(late, to_odd))
+        far = ones(more >= 2 * HF) * late
+        bad = far + up * (ones(rank >= CA) + ones(i_rank >= CI) + ones(p_rank >= width))
+        core = ones(more >= HF)
+        slot = jnp.where(late > 0, core * CF + HF + more - core * HF, (col % 2).astype(F32) * CF + rank)
+        f = jnp.where(up > 0, slot, 2.0 * CF).astype(jnp.int32)
+        a = jnp.where(up > 0, rank, float(CA)).astype(jnp.int32)
+        p = jnp.where(up > 0, p_rank, width).astype(jnp.int32)
+        i = jnp.where(up > 0, i_rank, float(CI)).astype(jnp.int32)
+        word = f + a * 32 + p * 1024 + i * 65536 + jnp.where(up > 0, 1 << 21, 0)
+        good = jnp.max(bad) < 0.5
+        tier = jnp.where(good, t, tier)
+        table = word if table is None else jnp.where(good, word, table)
+    tier_ref[0] = tier
+    tab_ref[...] = table
 
 
 def per_device(factor, adjoint, pattern):
-    fits = pl.pallas_call(
-        fits_kernel,
-        out_shape=jax.ShapeDtypeStruct((1,), jnp.int32),
+    tier, table = pl.pallas_call(
+        plan_kernel,
+        out_shape=(jax.ShapeDtypeStruct((1,), jnp.int32), jax.ShapeDtypeStruct((64, 64), jnp.int32)),
         in_specs=[pl.BlockSpec(memory_space=pltpu.VMEM)],
-        out_specs=pl.BlockSpec(memory_space=pltpu.SMEM),
+        out_specs=(pl.BlockSpec(memory_space=pltpu.SMEM), pl.BlockSpec(memory_space=pltpu.VMEM)),
     )(pattern)
-    return lax.cond(fits[0] > 0, sparse_device, dense_device, factor, adjoint, pattern)
+    ways = [functools.partial(sparse_device, t) for t in range(len(TIERS))] + [dense_device]
+    return lax.switch(tier[0], ways, factor, adjoint, pattern, table)
 
 
 def solution(mesh):

time: 87.4 us -> 69.3 us (0.79)
  Pallas kernels: 85.6 us -> 67.5 us
    pallas_call x2, Pallas kernels: 85.6 us -> 67.5 us  [the longest x1 65.5 us: sparse_device(): pl.pallas_call(functools.partial(sparse_kernel, TIERS[tier]), out_shape=j...]
where the time goes in v3:
time: 69.3 us; the launch traced here: 69.2 us
  Pallas kernels  67.5 us (97%)
  local copies, waits for them, and re-layouts  0.8 us (1%)
    pallas_call x1, Pallas kernels, sparse_device(): pl.pallas_call(functools.partial(sparse_kernel, TIERS[tier]), out_shape=j...  65.5 us
    pallas_call x1, Pallas kernels, per_device(): pl.pallas_call(plan_kernel, out_shape=(jax.ShapeDtypeStruct((1,), jnp.int...  1.97 us

profile of v3, /device:TPU:1, one launch (start us, length us, event | category | flops | bytes accessed | tf_op | source)
XLA Modules:
  0.0 69.2 jit_solution(9935920343227369313)
XLA Ops:
  0.0 0.0 copy-start
  0.0 2.0 %shard_map.40 = (s32[1]{0:T(128)}, s32[64,64]{1,0:T(8,128)S(1)}) custom-call(s32[64,64]{1,0:T(8,128)} %pat_ref.1), custom_call_target="tpu_custom_call" | custom-call | tf_op jit(solution)/shard_map/pallas_call | solution.py:760
  2.6 0.0 copy-done
  2.6 65.7 %conditional.1 = (bf16[512,512]{1,0:T(8,128)(2,1)S(1)}) conditional(s32[]{:T(128)} %bitcast.4, (bf16[2048,128]{1,0:T(8,128)(2,1)}, bf16[2048,128]{1,0:T(8,128)(2,1)}, s32[64,64]{1,0:T(8,128)S(1)}) %tuple.14, (bf16[2048,128]{1,0:T(8,128)(2,1)}, bf16[2048,128]{1,0:T(8,128)(2,1)}, s32[64,64]{1,0:T(8,128)S(1)}) %tuple.14, ...), branch_computations={%region_0.0_spmd, %region_1.0_spmd, %region_2.0_spmd} | conditional | flops 8589934592 | bytes 2097160 | solution.py:767
  2.7 65.5 %branch_0_fun.1 = bf16[512,512]{1,0:T(8,128)(2,1)S(1)} custom-call(bf16[16,128,128]{2,1,0:T(8,128)(2,1)} %bitcast.5, bf16[16,128,128]{2,1,0:T(8,128)(2,1)} %bitcast.7, s32[64,64]{1,0:T(8,128)S(1)} %get-tuple-element.29.tab_ref), custom_call_target="tpu_custom_call" | custom-call | flops 8589934592 | bytes 2097152 | tf_op jit(solution)/shard_map/cond/branch_0_fun/pallas_call | solution.py:671
  68.4 0.8 %copy.11 = bf16[512,512]{1,0:T(8,128)(2,1)} copy(bf16[512,512]{1,0:T(8,128)(2,1)S(1)} %get-tuple-element.40) | data formatting | bytes 1048576
Async XLA Ops:
  0.0 2.6 %copy-start = (s32[64,64]{1,0:T(8,128)S(1)}, s32[64,64]{1,0:T(8,128)}, u32[]{:S(2)}) copy-start(s32[64,64]{1,0:T(8,128)} %pat_ref.1) | copy-start | bytes 49156

commit v4 on v3

--- a/solution.py
+++ b/solution.py
@@ -195,6 +195,9 @@
         rows = pl.ds(pl.multiple_of(i * RC, RC), RC)
         img[rows, :] = product(rows, (-2, -1, 0, 1, 2))
 
+    for copy in started[:-3]:
+        copy.wait_send()
+    del started[:-3]
     wait_share(4)
     first(4, 1, 1)
     middle(3, 2, 2)
@@ -284,10 +287,10 @@
 
 
 def sparse_kernel(
-    caps, f_ref, a_ref, tab_ref, out_ref,
-    ownf, fs, fd, asl, at, acc, psend, prec, lsl, lx, img, ib, isend, relay, irec,
+    caps, f_hbm, a_hbm, tab_ref, out_ref,
+    f_ref, a_ref, ownf, fs, fd, asl, at, acc, psend, prec, lsl, lx, img, ib, isend, relay, irec,
     nxt, fenc, aenc, penc, ienc,
-    s_o, r_o, s_r, r_r, s_l, r_l, s_s, r_s, s_a, r_a, s_p, r_p, s_x, r_x, s_i, r_i,
+    s_in, s_o, r_o, s_r, r_r, s_l, r_l, s_s, r_s, s_a, r_a, s_p, r_p, s_x, r_x, s_i, r_i,
 ):
     CF, CA, CI, *widths = caps
     GROUPS = [(*span, width) for span, width in zip(SPANS, widths)]
@@ -295,8 +298,11 @@
     r, c, l = lax.axis_index("row"), lax.axis_index("col"), lax.axis_index("layer")
     z, k = c // 2, c % 2
 
+    def shr(v, n):
+        return lax.shift_right_logical(v, jnp.int32(n))
+
     def zpos(d):
-        return lax.rem(z + d + NZ, NZ)
+        return (z + d + NZ) & (NZ - 1)
 
     def at_z(d):
         return (r, zpos(d) * 2 + k, l)
@@ -319,6 +325,10 @@
             src_ref=src, dst_ref=dst, send_sem=ss, recv_sem=rs, device_id=dev, device_id_type=MESH
         )
 
+    fetch_a = pltpu.make_async_copy(a_hbm, a_ref, s_in.at[0])
+    fetch_f = pltpu.make_async_copy(f_hbm, f_ref, s_in.at[1])
+    fetch_a.start()
+    fetch_f.start()
     started = []
 
     def go(copy):
@@ -334,7 +344,8 @@
         lsl[g][GROUPS[g][2]] = nothing
 
     def field(row, col, shift, mask):
-        return lax.shift_right_logical(tab_ref[row, col], shift) & mask
+        word = tab_ref[row, col]
+        return (shr(word, shift) if shift else word) & mask
 
     def kept(row, col):
         return field(row, col, 21, 1)
@@ -348,7 +359,7 @@
             nxt[b] = nx
             return nx
 
-        lax.fori_loop(0, n, back, jnp.int32(0))
+        lax.fori_loop(0, n, back, jnp.int32(0), unroll=8)
 
         def chain(t, p):
             e = nxt[p]
@@ -358,7 +369,7 @@
         lax.fori_loop(0, cap, chain, jnp.int32(0))
 
     def f_dec(d, b):
-        return field(16 * l + b % 16, 16 * r + 2 * zpos(d) + b // 16, 0, 31)
+        return field(16 * l + (b & 15), 16 * r + 2 * zpos(d) + shr(b, 4), 0, 31)
 
     def p_dec(i, j):
         return field(16 * r + i, 4 * c + j, 10, 63)
@@ -369,8 +380,8 @@
 
         def back(t, carry):
             b = 63 - t
-            i, j = b // 4, b % 4
-            near = lax.rem(i // 2 - z - SPANS[0][0] + NZ, NZ) < SPANS[0][1]
+            i, j = shr(b, 2), b & 3
+            near = ((shr(b, 3) - z - SPANS[0][0] + NZ) & (NZ - 1)) < SPANS[0][1]
             one = kept(16 * r + i, 4 * c + j) > 0
             n0 = jnp.where(one & near, b, carry[0])
             n1 = jnp.where(one & jnp.logical_not(near), b, carry[1])
@@ -378,7 +389,7 @@
             nxt[72 + b] = n1
             return n0, n1
 
-        lax.fori_loop(0, 64, back, (jnp.int32(0), jnp.int32(0)))
+        lax.fori_loop(0, 64, back, (jnp.int32(0), jnp.int32(0)), unroll=8)
         for g in range(2):
             def chain(t, p, g=g):
                 e = nxt[72 * g + p]
@@ -387,36 +398,18 @@
 
             lax.fori_loop(0, GROUPS[g][2], chain, jnp.int32(0))
 
-    pl.semaphore_wait(barrier, len(partners))
-
-    own_col = remote(f_ref, ownf.at[k], s_o, r_o, sibling)
-    go(own_col)
+    picks(16, lambda b: kept(16 * l + b, 4 * c + r), aenc, 0, CA)
     picks(16, lambda b: kept(16 * l + b, 16 * r + 2 * z + k), fenc, 0, HF)
-
-    @pl.loop(0, HF)
-    def _(t):
-        fs[0][k * CF + t] = f_ref[fenc[t]]
-
-    def fslot(d, h):
-        return fs[d % NZ].at[pl.ds(k * CF + h * HF, HF)]
-
-    def ring_r(s, h):
-        return remote(fslot(-s, h), fslot(-s - 1, h), s_r.at[s, h], r_r.at[s, h], at_z(1))
-
-    def ring_l(s, h):
-        return remote(fslot(s, h), fslot(s + 1, h), s_l.at[s, h], r_l.at[s, h], at_z(-1))
-
-    def share(d, h):
-        return remote(fslot(d, h), fslot(d, h), s_s.at[d % NZ, h], r_s.at[d % NZ, h], sibling)
-
-    go(ring_r(0, 0))
-    go(ring_l(0, 0))
-
-    picks(16, lambda b: kept(16 * l + b, 4 * c + r), aenc, 0, CA)
+    fetch_a.wait()
 
     @pl.loop(0, CA)
     def _(t):
         asl[0][t] = a_ref[aenc[t]].T
+
+    fetch_f.wait()
+    for t in range(HF):
+        fs[0][k * CF + t] = f_ref[fenc[t]]
+    pl.semaphore_wait(barrier, len(partners))
 
     AH = CA // 2
 
@@ -429,11 +422,34 @@
         sl = pl.ds(h * AH, AH)
         return remote(asl[(-d) % 4].at[sl], asl[2].at[sl], s_a.at[2, h], r_a.at[2, h], at_y(d))
 
-    for h in range(2):
-        go(a_first(1, h))
-        go(a_first(-1, 1 - h))
-
-    over = lambda b: jnp.where(f_dec(0, b) % CF >= HF, 1, 0)
+    own_col = remote(f_ref, ownf.at[k], s_o, r_o, sibling)
+    go(a_first(1, 0))
+    go(a_first(-1, 1))
+    go(own_col)
+
+    def fslot(d, h):
+        return fs[d % NZ].at[pl.ds(k * CF + h * HF, HF)]
+
+    def ring_r(s, h):
+        return remote(fslot(-s, h), fslot(-s - 1, h), s_r.at[s, h], r_r.at[s, h], at_z(1))
+
+    def ring_l(s, h):
+        return remote(fslot(s, h), fslot(s + 1, h), s_l.at[s, h], r_l.at[s, h], at_z(-1))
+
+    def share(d, h):
+        return remote(fslot(d, h), fslot(d, h), s_s.at[d % NZ, h], r_s.at[d % NZ, h], sibling)
+
+    go(ring_r(0, 0))
+    go(ring_l(0, 0))
+
+    go(a_first(1, 1))
+    go(a_first(-1, 0))
+
+    def over(b):
+        slot = f_dec(0, b)
+        rest = jnp.where(slot >= CF, slot - CF, slot)
+        return jnp.where((rest >= HF) & (rest < CF), 1, 0)
+
     picks(32, over, fenc, HF, 2 * HF)
     ownf[k] = f_ref[...]
     own_col.wait_recv()
@@ -441,7 +457,7 @@
     @pl.loop(0, HF)
     def _(t):
         e = fenc[HF + k * HF + t]
-        fs[0][k * CF + HF + t] = ownf[e // 16, e % 16]
+        fs[0][k * CF + HF + t] = ownf[shr(e, 4), e & 15]
 
     go(ring_r(0, 1))
     go(ring_l(0, 1))
@@ -449,7 +465,7 @@
     p_tables()
     for d in (1, 2, 3):
         q = lax.rem(r + d, NR)
-        picks(16, lambda b: kept(16 * l + 4 * q + b // 4, 4 * c + b % 4), ienc, (d - 1) * CI, CI)
+        picks(16, lambda b: kept(16 * l + 4 * q + shr(b, 2), 4 * c + (b & 3)), ienc, (d - 1) * CI, CI)
 
     def arrive_r(s, h):
         ring_r(s, h).wait_recv()
@@ -469,24 +485,19 @@
 
     def a_expand(e):
         q = lax.rem(r + e, NR)
-
-        @pl.loop(0, 16, unroll=4)
-        def _(b):
-            dec = field(16 * l + b, 4 * c + q, 5, 31)
-            rows = pl.ds(pl.multiple_of(q * BLK, BLK), BLK)
-            cols = pl.ds(pl.multiple_of(b * BLK, BLK), BLK)
-            at[rows, cols] = asl[e][dec]
+        rows = pl.ds(pl.multiple_of(q * BLK, BLK), BLK)
+        for b in range(16):
+            at[rows, b * BLK : (b + 1) * BLK] = asl[e][field(16 * l + b, 4 * c + q, 5, 31)]
 
     def f_expand(d):
         w = zpos(d)
         for h in range(2):
             share(d, h).wait_recv()
 
-        @pl.loop(0, 32, unroll=4)
-        def _(b):
-            dec = f_dec(d, b)
-            rows = pl.ds(pl.multiple_of((b % 16) * BLK, BLK), BLK)
-            fd[w, b // 16, rows, :] = fs[d % NZ][dec]
+        for u in range(2):
+            for b in range(16):
+                dec = field(16 * l + b, 16 * r + 2 * w + u, 0, 31)
+                fd[w, u, pl.ds(b * BLK, BLK), :] = fs[d % NZ][dec]
 
     def first(g, d):
         w = zpos(d)
@@ -495,6 +506,13 @@
             for j in range(4):
                 acc[w * 8 + u * 4 + j] = res[j * BLK : (j + 1) * BLK, u * BLK : (u + 1) * BLK]
 
+    def first_of(d, e):
+        w, q = zpos(d), lax.rem(r + e, NR)
+        rows = at[pl.ds(pl.multiple_of(q * BLK, BLK), BLK), :]
+        res = jnp.dot(rows, jnp.concatenate([fd[w, 0], fd[w, 1]], axis=1), preferred_element_type=F32)
+        for u in range(2):
+            acc[w * 8 + u * 4 + q] = res[:, u * BLK : (u + 1) * BLK]
+
     def p_copy(g, d):
         n = GROUPS[g][2] // 4
         mine = pl.ds(lax.rem(l + d, NL) * n, n)
@@ -525,12 +543,12 @@
             tot = acc[e]
             for d in range(3):
                 tot = tot + prec[g][d, t].astype(F32)
-            row = 16 * r + e // 4
-            col = 4 * c + e % 4
-            ii = row * BLK + lax.broadcasted_iota(jnp.int32, (BLK, BLK), 0)
-            jj = col * BLK + lax.broadcasted_iota(jnp.int32, (BLK, BLK), 1)
+            row = 16 * r + shr(e, 2)
+            col = 4 * c + (e & 3)
+            ii = row * BLK + lax.broadcasted_iota(jnp.int32, (BLK, BLK), 1)
+            jj = col * BLK + lax.broadcasted_iota(jnp.int32, (BLK, BLK), 0)
             wt = jnp.where(ii < jj, 1.0, jnp.where(ii == jj, 0.5, 0.0)).astype(F32)
-            lsl[g][l * n + t] = (tot.T * wt).astype(BF16)
+            lsl[g][l * n + t] = (tot * wt).astype(BF16).T
 
         for d in (2, 1, 3):
             go(x_copy(g, d))
@@ -540,13 +558,14 @@
         for d in (1, 2, 3):
             x_copy(g, d).wait_recv()
 
-        @pl.loop(0, n * 8, unroll=4)
-        def _(b):
-            w, u, j = zpos(lo + b // 8), (b // 4) % 2, b % 4
-            dec = p_dec(2 * w + u, j)
-            lx[w, j, pl.ds(pl.multiple_of(u * BLK, BLK), BLK), :] = lsl[g][dec]
+        for o in range(n):
+            w = zpos(lo + o)
+            for u in range(2):
+                for j in range(4):
+                    lx[w, j, pl.ds(u * BLK, BLK), :] = lsl[g][p_dec(2 * w + u, j)]
 
     a_expand(0)
+    first_of(0, 0)
     a_first(1, 0).wait_recv()
     a_first(-1, 1).wait_recv()
     go(a_second(1))
@@ -557,17 +576,22 @@
     a_first(-1, 0).wait_recv()
     a_expand(1)
     a_expand(3)
+    first_of(0, 1)
+    first_of(0, 3)
     arrive_r(0, 1)
     arrive_l(0, 1)
     f_expand(1)
     f_expand(-1)
+    for e in (0, 1, 3):
+        first_of(1, e)
+        first_of(-1, e)
+    arrive_r(1, 0)
+    arrive_l(1, 0)
     a_second(1).wait_recv()
     a_second(-1).wait_recv()
     a_expand(2)
-    arrive_r(1, 0)
-    arrive_l(1, 0)
     for d in (0, 1, -1):
-        first(0, d)
+        first_of(d, 2)
     arrive_r(1, 1)
     arrive_l(1, 1)
     for d in (2, -2):
@@ -671,10 +695,10 @@
     return pl.pallas_call(
         functools.partial(sparse_kernel, TIERS[tier]),
         out_shape=jax.ShapeDtypeStruct((512, 512), BF16),
-        in_specs=[vmem, vmem, pl.BlockSpec(memory_space=pltpu.SMEM)],
+        in_specs=[pl.BlockSpec(memory_space=pl.ANY)] * 2 + [pl.BlockSpec(memory_space=pltpu.SMEM)],
         out_specs=vmem,
         scratch_shapes=[
-            blocks(2, 16),
+            blocks(16), blocks(16), blocks(2, 16),
             [blocks(2 * CF + 1) for _ in range(NZ)],
             scratch((NZ, 2, ROWS, BLK), BF16),
             [blocks(CA + 1) for _ in range(NR)],
@@ -690,7 +714,7 @@
             [blocks(CI // 2) for _ in range(4)],
             [blocks(CI) for _ in range(4)],
             ints(144), ints(3 * CF), ints(CA), [ints(n) for n in caps], ints(3 * CI),
-            dma, dma,
+            dma((2,)), dma, dma,
             dma((4, 2)), dma((4, 2)), dma((4, 2)), dma((4, 2)),
             dma((NZ, 2)), dma((NZ, 2)),
             dma((4, 2)), dma((4, 2)),

time: 69.3 us -> 81.3 us (1.17)
  Pallas kernels: 67.5 us -> 78.9 us
    pallas_call x1, Pallas kernels: 65.5 us -> 77 us  [sparse_device(): pl.pallas_call(functools.partial(sparse_kernel, TIERS[tier]), out_shape=j...]
where the time goes in v4:
time: 81.3 us; the launch traced here: 81.2 us
  Pallas kernels  78.9 us (97%)
    pallas_call x1, Pallas kernels, sparse_device(): pl.pallas_call(functools.partial(sparse_kernel, TIERS[tier]), out_shape=j...  77 us
    pallas_call x1, Pallas kernels, per_device(): pl.pallas_call(plan_kernel, out_shape=(jax.ShapeDtypeStruct((1,), jnp.int...  1.97 us

profile of v4, /device:TPU:1, one launch (start us, length us, event | category | flops | bytes accessed | tf_op | source)
XLA Modules:
  0.0 81.2 jit_solution(10321660048757460496)
XLA Ops:
  0.0 0.0 copy-start
  0.0 2.0 %shard_map.40 = (s32[1]{0:T(128)}, s32[64,64]{1,0:T(8,128)S(1)}) custom-call(s32[64,64]{1,0:T(8,128)} %pat_ref.1), custom_call_target="tpu_custom_call" | custom-call | tf_op jit(solution)/shard_map/pallas_call | solution.py:784
  2.6 0.0 copy-done
  2.6 77.7 %conditional.1 = (bf16[512,512]{1,0:T(8,128)(2,1)S(1)}) conditional(s32[]{:T(128)} %bitcast.4, (bf16[2048,128]{1,0:T(8,128)(2,1)}, bf16[2048,128]{1,0:T(8,128)(2,1)}, s32[64,64]{1,0:T(8,128)S(1)}) %tuple.14, (bf16[2048,128]{1,0:T(8,128)(2,1)}, bf16[2048,128]{1,0:T(8,128)(2,1)}, s32[64,64]{1,0:T(8,128)S(1)}) %tuple.14, ...), branch_computations={%region_0.0_spmd, %region_1.0_spmd, %region_2.0_spmd} | conditional | flops 8589934592 | bytes 2097160 | solution.py:791
  2.9 77.0 %branch_1_fun.1 = bf16[512,512]{1,0:T(8,128)(2,1)S(1)} custom-call(bf16[16,128,128]{2,1,0:T(8,128)(2,1)} %bitcast.6, bf16[16,128,128]{2,1,0:T(8,128)(2,1)} %bitcast.8, s32[64,64]{1,0:T(8,128)S(1)} %get-tuple-element.32.tab_ref), custom_call_target="tpu_custom_call" | custom-call | flops 8589934592 | bytes 2097152 | tf_op jit(solution)/shard_map/cond/branch_1_fun/pallas_call | solution.py:695
  80.4 0.8 copy.11
Async XLA Ops:
  0.0 2.6 %copy-start = (s32[64,64]{1,0:T(8,128)S(1)}, s32[64,64]{1,0:T(8,128)}, u32[]{:S(2)}) copy-start(s32[64,64]{1,0:T(8,128)} %pat_ref.1) | copy-start | bytes 49156

commit v5 on v4

--- a/solution.py
+++ b/solution.py
@@ -283,7 +283,7 @@
 
 
 SPANS = ((-2, 5), (3, 3))
-TIERS = ((6, 8, 8, 16, 12), (8, 12, 12, 20, 16))
+TIERS = ((6, 8, 8, 16, 12), (8, 10, 10, 20, 12))
 
 
 def sparse_kernel(

time: 81.3 us -> 66.5 us (0.82)
  Pallas kernels: 78.9 us -> 64.6 us
    pallas_call x1, Pallas kernels: 77 us -> 62.6 us  [sparse_device(): pl.pallas_call(functools.partial(sparse_kernel, TIERS[tier]), out_shape=j...]
where the time goes in v5:
time: 66.5 us; the launch traced here: 66.3 us
  Pallas kernels  64.6 us (97%)
  local copies, waits for them, and re-layouts  0.8 us (1%)
  between operations  0.67 us (1%)
    pallas_call x1, Pallas kernels, sparse_device(): pl.pallas_call(functools.partial(sparse_kernel, TIERS[tier]), out_shape=j...  62.6 us
    pallas_call x1, Pallas kernels, per_device(): pl.pallas_call(plan_kernel, out_shape=(jax.ShapeDtypeStruct((1,), jnp.int...  1.97 us

profile of v5, /device:TPU:1, one launch (start us, length us, event | category | flops | bytes accessed | tf_op | source)
XLA Modules:
  0.0 66.3 jit_solution(4025770283881737633)
XLA Ops:
  0.0 0.0 copy-start
  0.0 2.0 %shard_map.40 = (s32[1]{0:T(128)}, s32[64,64]{1,0:T(8,128)S(1)}) custom-call(s32[64,64]{1,0:T(8,128)} %pat_ref.1), custom_call_target="tpu_custom_call" | custom-call | tf_op jit(solution)/shard_map/pallas_call | solution.py:784
  2.6 0.0 copy-done
  2.6 62.9 %conditional.1 = (bf16[512,512]{1,0:T(8,128)(2,1)S(1)}) conditional(s32[]{:T(128)} %bitcast.4, (bf16[2048,128]{1,0:T(8,128)(2,1)}, bf16[2048,128]{1,0:T(8,128)(2,1)}, s32[64,64]{1,0:T(8,128)S(1)}) %tuple.14, (bf16[2048,128]{1,0:T(8,128)(2,1)}, bf16[2048,128]{1,0:T(8,128)(2,1)}, s32[64,64]{1,0:T(8,128)S(1)}) %tuple.14, ...), branch_computations={%region_0.0_spmd, %region_1.0_spmd, %region_2.0_spmd} | conditional | flops 8589934592 | bytes 2097160 | solution.py:791
  2.7 62.6 %branch_0_fun.1 = bf16[512,512]{1,0:T(8,128)(2,1)S(1)} custom-call(bf16[16,128,128]{2,1,0:T(8,128)(2,1)} %bitcast.5, bf16[16,128,128]{2,1,0:T(8,128)(2,1)} %bitcast.7, s32[64,64]{1,0:T(8,128)S(1)} %get-tuple-element.29.tab_ref), custom_call_target="tpu_custom_call" | custom-call | flops 8589934592 | bytes 2097152 | tf_op jit(solution)/shard_map/cond/branch_0_fun/pallas_call | solution.py:695
  65.5 0.8 %copy.11 = bf16[512,512]{1,0:T(8,128)(2,1)} copy(bf16[512,512]{1,0:T(8,128)(2,1)S(1)} %get-tuple-element.40) | data formatting | bytes 1048576
Async XLA Ops:
  0.0 2.6 %copy-start = (s32[64,64]{1,0:T(8,128)S(1)}, s32[64,64]{1,0:T(8,128)}, u32[]{:S(2)}) copy-start(s32[64,64]{1,0:T(8,128)} %pat_ref.1) | copy-start | bytes 49156
